TPU v7x, 32 devices: a whole 2x2x4 slice. The times are simulated.
32 devices in a mesh: gx: 4 (over x, core), gy: 8 (over z, y).
Axes of the slice: x: 2, y: 2, z: 4, core: 2. Of those that a mesh axis runs over, the one named last changes fastest.
Arguments:
- state: float32 [2, 8, 128, 512], P(None, None, 'gy', 'gx'), may hold values from 0 to 1, as said below
- previous: float32 [2, 8, 128, 512], P(None, None, 'gy', 'gx'), may hold values from 0 to 1
- feed: float32 [8, 128, 512], P(None, 'gy', 'gx'), may hold values from 0.01 to 0.1
- kill: float32 [8, 128, 512], P(None, 'gy', 'gx'), may hold values from 0.03 to 0.1
Outputs:
- correction: float32 [2, 8, 128, 512], P(None, None, 'gy', 'gx')
Inputs may be any that keep to these rules, and one draw needn't show every extreme that they name: `state`: u and v of every cell lie in the stated range.
All inputs are finite; a program needn't handle non-finite values.
Results may differ from a plain program's by a relative error of at most 0.0001.
Values sent between devices are 32-bit elements; how exact they have to be, the bound alone decides.
No kernel may reach another device: no remote copies, remote signals or barrier semaphores. Data moves between devices by JAX's collectives and lax.ppermute only.
A program may use at most 128 MiB of HBM per device.

v0:
```python
import functools

import jax
import jax.numpy as jnp
from jax import lax
from jax.experimental import pallas as pl
from jax.experimental.pallas import tpu as pltpu
from jax.sharding import PartitionSpec as P

DIFF = (40.0, 20.0)
INV_STEP = 2.0
LOWER = 0.25

_CENTRE = (1.0 + LOWER) / 2.0
_HALF = (1.0 - LOWER) / 2.0
_SIGMA = _CENTRE / _HALF
_RHO0 = 1.0 / _SIGMA
_RHO1 = 1.0 / (2.0 * _SIGMA - _RHO0)
_RHO2 = 1.0 / (2.0 * _SIGMA - _RHO1)

Z = 8
X = 128
HALO0 = 4
WIDE = 18
PER = X // WIDE
EDGE = 3
CHUNK = 4

LO1, HI1 = -4, 8
LO2, HI2 = -2, 3
LO_UP, HI_UP = -3, 7
SIZE1, SIZE2, SIZE_UP = HI1 - LO1 + 2, HI2 - LO2 + 2, HI_UP - LO_UP + 2
OWN = 4


def lane_of():
    return lax.broadcasted_iota(jnp.int32, (1, Z, X), 2)


def sub_of():
    return lax.broadcasted_iota(jnp.int32, (1, Z, X), 1)


def roll_x(tile, shift):
    shift = shift % X
    return pltpu.roll(tile, shift, 2) if shift else tile


def roll_z(tile, shift):
    shift = shift % Z
    return pltpu.roll(tile, shift, 1) if shift else tile


def rows_loop(lo, hi, body, step=CHUNK):
    full = (hi - lo) // step
    if full == 1:
        body(lo, step)
    elif full > 1:

        def trip(i, carry):
            body(lo + i * step, step)
            return carry

        lax.fori_loop(0, full, trip, 0)
    rest = hi - lo - full * step
    if rest:
        body(hi - rest, rest)


def neighbour_sums(read, r, n, k):
    lane = lane_of()
    low, high = lane < k, lane >= X - k
    centre = [read(t, r, n) for t in (0, 1)]
    right = [roll_x(c, k) for c in centre]
    left = [roll_x(c, -k) for c in centre]
    sums = []
    for t in (0, 1):
        c = centre[t]
        along_x = jnp.where(low, right[1 - t], right[t]) + jnp.where(high, left[1 - t], left[t])
        along_y = read(t, r - 1, n) + read(t, r + 1, n)
        along_z = 2.0 * roll_z(c, k) if 2 * k == Z else roll_z(c, k) + roll_z(c, -k)
        sums.append(along_x + along_y + along_z)
    return centre, sums


def jacobian(u, v, f, k, level):
    scale = 0.25**level
    product = u * v
    squared = v * v
    first = INV_STEP + squared + f + 6.0 * DIFF[0] * scale
    second = INV_STEP + f + k - 2.0 * product + 6.0 * DIFF[1] * scale
    return 2.0 * product, squared, 1.0 / first, 1.0 / second, first, second


def cheb_step(level, keep, source, target, d, r, n, carry, gain):
    scale = 0.25**level
    k = 1 << level
    u, nb_u = neighbour_sums(lambda t, a, m: source[0, t, pl.ds(a, m)], r, n, k)
    v, nb_v = neighbour_sums(lambda t, a, m: source[1, t, pl.ds(a, m)], r, n, k)
    rows = pl.ds(r, n)
    for t in (0, 1):
        cross, squared, inv_u, inv_v = (keep[i, t, rows] for i in range(4))
        res_u = inv_u * (keep[4, t, rows] - cross * v[t] + DIFF[0] * scale * nb_u[t]) - u[t]
        res_v = inv_v * (keep[5, t, rows] + squared * u[t] + DIFF[1] * scale * nb_v[t]) - v[t]
        du, dv = gain * res_u, gain * res_v
        if carry is not None:
            du = du + carry * d[0, t, rows]
            dv = dv + carry * d[1, t, rows]
        d[0, t, rows] = du
        d[1, t, rows] = dv
        target[0, t, rows] = u[t] + du
        target[1, t, rows] = v[t] + dv


def residual(level, keep, diag, source, r, n):
    scale = 0.25**level
    k = 1 << level
    u, nb_u = neighbour_sums(lambda t, a, m: source[0, t, pl.ds(a, m)], r, n, k)
    v, nb_v = neighbour_sums(lambda t, a, m: source[1, t, pl.ds(a, m)], r, n, k)
    rows = pl.ds(r, n)
    first, second = [], []
    for t in (0, 1):
        first.append(
            keep[4, t, rows] - diag[0, t, rows] * u[t] - keep[0, t, rows] * v[t] + DIFF[0] * scale * nb_u[t]
        )
        second.append(
            keep[5, t, rows] - diag[1, t, rows] * v[t] + keep[1, t, rows] * u[t] + DIFF[1] * scale * nb_v[t]
        )
    return first, second


CARRY1 = _RHO1 * _RHO0
CARRY2 = _RHO2 * _RHO1


def write_gains(spread, out):
    row = lax.broadcasted_iota(jnp.int32, (Z, X), 0)
    for level in range(3):
        top = jnp.max(jnp.where(row == level, spread, 0.0), axis=0, keepdims=True)
        tau = 1.0 / (1.0 + jnp.broadcast_to(top, (Z, X)))
        for i, factor in enumerate((1.0 / _CENTRE, 2.0 * _RHO1 / _HALF, 2.0 * _RHO2 / _HALF)):
            out[3 * level + i] = factor * tau


def pair_rows(value):
    n = value.shape[0] // 2
    pairs = value.reshape(n, 2, Z, X)
    return pairs[:, 0] + pairs[:, 1]


def restrict_01(first, second):
    lane, sub = lane_of(), sub_of()
    across = []
    for value in (first, second):
        a, b = value[0:1], value[1:2]
        across.append(jnp.where((lane & 1) == 0, a + roll_x(a, -1), b + roll_x(b, 1)))
    a, b = across
    return 0.125 * jnp.where((sub & 1) == 0, a + roll_z(a, -1), b + roll_z(b, 1))


def restrict_12(groups):
    lane, sub = lane_of(), sub_of()
    out = None
    for p, value in enumerate(groups):
        value = value + roll_x(value, 1 if p & 1 else -1)
        value = value + roll_x(value, 2 if p & 2 else -2)
        out = value if out is None else jnp.where((lane & 3) == p, value, out)
    return 0.125 * (out + jnp.where((sub & 2) == 0, roll_z(out, -2), roll_z(out, 2)))


def spread_x(tile, k, phase):
    return jnp.where((lane_of() & k) == phase, tile, roll_x(tile, -k if phase else k))


def packed_jacobian(uv, fk, level):
    scale = 0.25**level
    even = (sub_of() & 1) == 0
    u, v = jnp.where(even, uv, roll_z(uv, 1)), jnp.where(even, roll_z(uv, -1), uv)
    f, k = jnp.where(even, fk, roll_z(fk, 1)), jnp.where(even, roll_z(fk, -1), fk)
    product, squared = u * v, v * v
    diag = jnp.where(
        even,
        INV_STEP + squared + f + 6.0 * DIFF[0] * scale,
        INV_STEP + f + k - 2.0 * product + 6.0 * DIFF[1] * scale,
    )
    return 1.0 / diag, jnp.where(even, -2.0 * product, squared), diag


def packed_spread(uv, fk, level):
    scale = 0.25**level
    even = (sub_of() & 1) == 0
    inverse, other, _ = packed_jacobian(uv, fk, level)
    return jnp.where(even, 6.0 * DIFF[0] * scale - other, 6.0 * DIFF[1] * scale + other) * inverse


def packed_terms(source, g, n, level):
    k = 1 << level
    lane, sub = lane_of(), sub_of()
    even = (sub & 1) == 0
    first, last = (lane & (k - 1)) == 0, (lane & (k - 1)) == k - 1
    low, high = lane < k, lane >= X - k
    diff = jnp.where(even, DIFF[0] * 0.25**level, DIFF[1] * 0.25**level)
    wide = [source[t, pl.ds(g - 1, n + 2)] for t in (0, 1)]
    centre = [w[1 : n + 1] for w in wide]
    right = [roll_x(c, k) for c in centre]
    left = [roll_x(c, -k) for c in centre]
    out = []
    for t in (0, 1):
        c, w = centre[t], wide[t]
        total = jnp.where(low, right[1 - t], right[t]) + jnp.where(high, left[1 - t], left[t])
        if k == 2:
            ahead, back = roll_x(w, 1), roll_x(w, -1)
            total = total + jnp.where(first, back[0:n], ahead[1 : n + 1])
            total = total + jnp.where(last, ahead[2 : n + 2], back[1 : n + 1])
            total = total + roll_z(c, 2) + roll_z(c, -2)
        else:
            total = total + jnp.where(first, roll_x(w[0:n], -(k - 1)), roll_x(c, 1))
            total = total + jnp.where(last, roll_x(w[2 : n + 2], k - 1), roll_x(c, -1))
            total = total + 2.0 * roll_z(c, 4)
        other = jnp.where(even, roll_z(c, -1), roll_z(c, 1))
        out.append((c, other, diff * total))
    return out


def packed_first(coef, shift, b, target, d, g, n, gain):
    for t in (0, 1):
        value = gain * coef[0, t, pl.ds(g + shift, n)] * b[t, pl.ds(g + shift, n)]
        d[t, pl.ds(g, n)] = value
        target[t, pl.ds(g, n)] = value


def packed_step(level, coef, shift, b, source, target, d, g, n, carry, gain):
    for t, (c, other, spread) in enumerate(packed_terms(source, g, n, level)):
        at = pl.ds(g + shift, n)
        res = coef[0, t, at] * (b[t, at] + coef[1, t, at] * other + spread) - c
        delta = gain * res
        if carry is not None:
            delta = delta + carry * d[t, pl.ds(g, n)]
        d[t, pl.ds(g, n)] = delta
        target[t, pl.ds(g, n)] = c + delta


def plane(ref, f, y, rows):
    return ref[pl.ds(f * Z * rows + y, Z, stride=rows), :]


FIELDS1 = 6 * HALO0


def is_even(axis):
    return lax.rem(lax.axis_index(axis), 2) == 0


def prev_of(even, first, second, at):
    return jnp.where(even, first[at], second[at])


def next_of(even, first, second, at):
    return jnp.where(even, second[at], first[at])


def first_kernel(rows, state, previous, feed, kill, first, second, main, coarse, packet, *scratch):
    sources, sems = scratch[:4], scratch[4]
    copies = [
        pltpu.make_async_copy(ref, held, sems.at[i])
        for i, (ref, held) in enumerate(zip((state, previous, feed, kill), sources))
    ]
    for copy in copies:
        copy.start()
    for copy in copies:
        copy.wait()
    even = is_even("gy")
    state, previous, feed, kill = sources
    fields = [(state, 0), (state, 1), (previous, 0), (previous, 1), (feed, 0), (kill, 0)]
    for i, (ref, f) in enumerate(fields):
        for y in range(rows):
            main[i, y] = plane(ref, f, y, rows)
        top, bottom = main[i, 0:HALO0], main[i, rows - HALO0 : rows]
        at = slice(i * HALO0, (i + 1) * HALO0)
        first[at] = jnp.where(even, top, bottom)
        second[at] = jnp.where(even, bottom, top)
    u, v, f, k = (main[i] for i in (0, 1, 4, 5))
    sums = [pair_rows(value) for value in (u, v, f, k)]
    pairs = []
    for p in (0, 1):
        values = [
            restrict_01(sums[2 * p][2 * g : 2 * g + 2], sums[2 * p + 1][2 * g : 2 * g + 2]) for g in range(OWN)
        ]
        pairs.append(jnp.concatenate(values, axis=0))
        coarse[p * OWN : (p + 1) * OWN] = pairs[p]
        for ref in (first, second):
            ref[FIELDS1 + p * OWN : FIELDS1 + (p + 1) * OWN] = pairs[p]

    row = lax.broadcasted_iota(jnp.int32, (Z, X), 0)
    cross, squared, inv_u, inv_v, _, _ = jacobian(u, v, f, k, 0)
    tops = [jnp.max(jnp.maximum((6.0 * DIFF[0] + cross) * inv_u, (6.0 * DIFF[1] + squared) * inv_v), axis=0)]
    tops.append(jnp.max(packed_spread(*pairs, 1), axis=0))
    uv, fk = (restrict_12([pair[j : j + 1] for j in range(OWN)]) for pair in pairs)
    tops.append(packed_spread(uv, fk, 2)[0])
    both = jnp.where((sub_of() & 2) == 0, uv, fk)[0]
    result = jnp.zeros((Z, X), jnp.float32)
    for level, top in enumerate(tops):
        top = jnp.max(jnp.max(top, axis=1, keepdims=True), axis=0, keepdims=True)
        result = jnp.where(row == level, jnp.broadcast_to(top, (Z, X)), result)
    for c in range(packet.shape[0] // 2):
        packet[2 * c] = both
        packet[2 * c + 1] = result


def around(across, count, gathered, chunk):
    lane = lane_of()
    gx, gy = lax.axis_index("gx"), lax.axis_index("gy")
    columns = [lax.rem(gx + i + across, across) * count for i in (-1, 0, 1)]
    out = [[], []]
    for q in range(LO2, HI2):
        row = lax.rem(gy + q + 4 * count, count)
        left, centre, right = (gathered[pl.ds((column + row) * chunk, 1)] for column in columns)
        out[0].append(centre)
        out[1].append(jnp.where(lane < X // 2, right, left))
    return [jnp.concatenate(groups, axis=0) for groups in out]


GROUPS1 = HI1 - LO1
GROUPS2 = HI2 - LO2


def pack_slots(parts, width):
    lane = lane_of()
    left, right = None, None
    for j, part in enumerate(parts):
        a, b = roll_x(part, width * j), roll_x(part, width + width * j)
        left = a if left is None else jnp.where(lane >= width * j, a, left)
        right = b if right is None else jnp.where(lane >= width * j, b, right)
    return left, right


def unpack_slot(from_left, from_right, j, width):
    return jnp.where(lane_of() < X // 2, roll_x(from_right, -width * j), roll_x(from_left, X - width - width * j))


def pack_x_kernel(rows, main, coarse, y_first, y_second, first, second, held):
    even = is_even("gy")
    total = rows + 2 * HALO0
    share = held.shape[0] // PER
    for i in range(6):
        strip = slice(i * HALO0, (i + 1) * HALO0)
        held[i * total : i * total + HALO0] = prev_of(even, y_first, y_second, strip)
        held[i * total + HALO0 : i * total + HALO0 + rows] = main[i]
        held[i * total + HALO0 + rows : (i + 1) * total] = next_of(even, y_first, y_second, strip)
    for p in (0, 1):
        to = 6 * total + p * GROUPS1
        strip = slice(FIELDS1 + p * OWN, FIELDS1 + (p + 1) * OWN)
        held[to : to + OWN] = prev_of(even, y_first, y_second, strip)
        held[to + OWN : to + 2 * OWN] = coarse[p * OWN : (p + 1) * OWN]
        held[to + 2 * OWN : to + 3 * OWN] = next_of(even, y_first, y_second, strip)
    left, right = pack_slots([held[j * share : (j + 1) * share] for j in range(PER)], WIDE)
    even = is_even("gx")
    first[...] = jnp.where(even, left, right)
    second[...] = jnp.where(even, right, left)


HALO1 = X // (2 * OWN)
EDGES = OWN + 1


def level0_kernel(
    rows, main, y_first, y_second, x_first, x_second, gathered, own, first, second, keep, gain_out, fields, other, d, diag
):
    even, even_x = is_even("gy"), is_even("gx")
    total = rows + 2 * HALO0
    share = (6 * total + 2 * GROUPS1) // PER
    top = gathered[1]
    for c in range(1, gathered.shape[0] // 2):
        top = jnp.maximum(top, gathered[2 * c + 1])
    write_gains(top, gain_out)
    g0, g1, g2 = (gain_out[i] for i in range(3))
    for i in range(6):
        strip = slice(i * HALO0, (i + 1) * HALO0)
        fields[i, 0, 0:HALO0] = prev_of(even, y_first, y_second, strip)
        fields[i, 0, HALO0 : HALO0 + rows] = main[i]
        fields[i, 0, HALO0 + rows : total] = next_of(even, y_first, y_second, strip)
        for j in range(PER):
            lo, hi = max(i * total, j * share), min((i + 1) * total, (j + 1) * share)
            if lo < hi:
                strip = slice(lo - j * share, hi - j * share)
                left, right = prev_of(even_x, x_first, x_second, strip), next_of(even_x, x_first, x_second, strip)
                fields[i, 1, lo - i * total : hi - i * total] = unpack_slot(left, right, j, WIDE)
    here = keep.at[6:8]

    def setup(r, n):
        at = pl.ds(r, n)
        u, nb_u = neighbour_sums(lambda t, a, m: fields[0, t, pl.ds(a, m)], r, n, 1)
        v, nb_v = neighbour_sums(lambda t, a, m: fields[1, t, pl.ds(a, m)], r, n, 1)
        for t in (0, 1):
            f, k = fields[4, t, at], fields[5, t, at]
            cross, squared, inv_u, inv_v, first, second = jacobian(u[t], v[t], f, k, 0)
            react = u[t] * squared
            b_u = (
                DIFF[0] * (nb_u[t] - 6.0 * u[t])
                - INV_STEP * (u[t] - fields[2, t, at])
                - react
                + f * (1.0 - u[t])
            )
            b_v = (
                DIFF[1] * (nb_v[t] - 6.0 * v[t]) - INV_STEP * (v[t] - fields[3, t, at]) + react - (f + k) * v[t]
            )
            for i, value in enumerate((cross, squared, inv_u, inv_v, b_u, b_v)):
                keep[i, t, at] = value
            diag[0, t, at] = first
            diag[1, t, at] = second
            for i, value in enumerate((g0 * inv_u * b_u, g0 * inv_v * b_v)):
                d[i, t, at] = value
                keep[6 + i, t, at] = value

    rows_loop(1, total - 1, setup)
    rows_loop(2, total - 2, lambda r, n: cheb_step(0, keep, here, other, d, r, n, CARRY1, g1))
    rows_loop(3, total - 3, lambda r, n: cheb_step(0, keep, other, here, d, r, n, CARRY2, g2))

    def down(r, n):
        res = residual(0, keep, diag, here, r, n)
        out = (r - HALO0) // 4
        for t in (0, 1):
            value = restrict_01(pair_rows(res[0][t]), pair_rows(res[1][t]))
            own[t, pl.ds(out, 1)] = value
            if t == 0:
                first[pl.ds(out, 1)] = value
                second[pl.ds(out, 1)] = value

    rows_loop(HALO0, HALO0 + rows, down, 4)

    lane = lane_of()
    sides = None
    for j in range(OWN):
        value = roll_x(own[1, j : j + 1], HALO1 + 2 * HALO1 * j)
        sides = value if sides is None else jnp.where(lane // (2 * HALO1) == j, value, sides)
    edges = []
    for start in (HALO0, HALO0 + rows - EDGE):
        halo = None
        for i in (0, 1):
            for j in range(EDGE):
                at = i * EDGE + j
                value = roll_x(keep[6 + i, 1, start + j : start + j + 1], 4 + 8 * at)
                halo = value if halo is None else jnp.where((lane >> 3) == at, value, halo)
        edges.append([keep[6, 0, start : start + EDGE], keep[7, 0, start : start + EDGE], halo])
    top, bottom = (jnp.concatenate(parts, axis=0) for parts in edges)
    for ref in (first, second):
        ref[OWN : OWN + 1] = sides
    first[EDGES : EDGES + 2 * EDGE + 1] = jnp.where(even, top, bottom)
    second[EDGES : EDGES + 2 * EDGE + 1] = jnp.where(even, bottom, top)


def coarse_kernel(
    across, count, rows, coarse, y_first, y_second, x_first, x_second, gathered, gain, coef1, coef2, fields
):
    del gain
    even, even_x = is_even("gy"), is_even("gx")
    share = (6 * (rows + 2 * HALO0) + 2 * GROUPS1) // PER
    base = 6 * (rows + 2 * HALO0) - (PER - 1) * share
    for p in (0, 1):
        to = p * GROUPS1
        strip = slice(FIELDS1 + p * OWN, FIELDS1 + (p + 1) * OWN)
        fields[0, to : to + OWN] = prev_of(even, y_first, y_second, strip)
        fields[0, to + OWN : to + 2 * OWN] = coarse[p * OWN : (p + 1) * OWN]
        fields[0, to + 2 * OWN : to + 3 * OWN] = next_of(even, y_first, y_second, strip)
    strip = slice(base, share)
    left, right = prev_of(even_x, x_first, x_second, strip), next_of(even_x, x_first, x_second, strip)
    fields[1] = unpack_slot(left, right, PER - 1, WIDE)
    for t in (0, 1):
        for i, value in enumerate(packed_jacobian(fields[t, 0:GROUPS1], fields[t, GROUPS1 : 2 * GROUPS1], 1)):
            coef1[i, t, 1 : SIZE1 - 1] = value

    sub = sub_of()
    for t, both in enumerate(around(across, count, gathered, 2)):
        uv = jnp.where((sub & 2) == 0, both, roll_z(both, 2))
        fk = jnp.where((sub & 2) == 0, roll_z(both, -2), both)
        inverse, other, _ = packed_jacobian(uv, fk, 2)
        coef2[0, t, 1 : SIZE2 - 1] = inverse
        coef2[1, t, 1 : SIZE2 - 1] = other


def level1_kernel(own, first, second, coef1, gain, packet, keep, y1, d1):
    b1, x1 = keep.at[0], keep.at[1]
    even = is_even("gy")
    for t in (0, 1):
        b1[t, 1 + OWN : 1 + 2 * OWN] = own[t]
        for take, at in ((prev_of, 1), (next_of, 1 + 2 * OWN)):
            if t == 0:
                b1[t, at : at + OWN] = take(even, first, second, slice(0, OWN))
            else:
                sides = take(even, first, second, slice(OWN, OWN + 1))
                for j in range(OWN):
                    b1[t, at + j : at + j + 1] = roll_x(sides, -(HALO1 + 2 * HALO1 * j))
    g0, g1, g2 = (gain[3 + i] for i in range(3))
    n = GROUPS1
    packed_first(coef1, 0, b1, x1, d1, 1, n, g0)
    packed_step(1, coef1, 0, b1, x1, y1, d1, 1, n, CARRY1, g1)
    packed_step(1, coef1, 0, b1, y1, x1, d1, 1, n, CARRY2, g2)
    here = pl.ds(1 + OWN, OWN)
    c, other, spread = packed_terms(x1, 1 + OWN, OWN, 1)[0]
    res = b1[0, here] - coef1[2, 0, here] * c + coef1[1, 0, here] * other + spread
    value = restrict_12([res[j : j + 1] for j in range(OWN)])
    for c in range(packet.shape[0]):
        packet[c : c + 1] = value


def rest_kernel(
    across, count, gathered, gain, coef1, coef2, keep0, keep1, first, second, out, d1, b2, x2, y2, d2, xu, yu, x0, y0, d0
):
    rows = out.shape[0] // (2 * Z)
    even = (sub_of() & 1) == 0
    b1, x1 = keep1.at[0], keep1.at[1]

    for t, groups in enumerate(around(across, count, gathered, 1)):
        b2[t, 1 : SIZE2 - 1] = groups

    n = HI2 - LO2
    g0, g1, g2 = (gain[6 + i] for i in range(3))
    packed_first(coef2, 0, b2, x2, d2, 1, n, g0)
    packed_step(2, coef2, 0, b2, x2, y2, d2, 1, n, CARRY1, g1)
    packed_step(2, coef2, 0, b2, y2, x2, d2, 1, n, CARRY2, g2)
    packed_step(2, coef2, 0, b2, x2, y2, d2, 1, n, None, g0)
    packed_step(2, coef2, 0, b2, y2, x2, d2, 1, n, CARRY1, g1)
    packed_step(2, coef2, 0, b2, x2, y2, d2, 1, n, CARRY2, g2)

    g0, g1, g2 = (gain[3 + i] for i in range(3))
    shift = LO_UP - LO1
    for t in (0, 1):
        for g in range(LO_UP, HI_UP):
            p = g % 4
            value = y2[t, g // 4 - LO2 + 1 : g // 4 - LO2 + 2]
            value = spread_x(spread_x(value, 1, p & 1), 2, p & 2)
            at = g - LO_UP + 1
            xu[t, at : at + 1] = x1[t, at + shift : at + shift + 1] + value
    n = HI_UP - LO_UP
    packed_step(1, coef1, shift, b1, xu, yu, d1, 1, n, None, g0)
    packed_step(1, coef1, shift, b1, yu, xu, d1, 1, n, CARRY1, g1)
    packed_step(1, coef1, shift, b1, xu, yu, d1, 1, n, CARRY2, g2)

    g0, g1, g2 = (gain[i] for i in range(3))
    last = EDGES + 2 * EDGE
    even_y = is_even("gy")
    for i in (0, 1):
        for at, take in ((HALO0 - EDGE, prev_of), (HALO0 + rows, next_of)):
            strip = slice(EDGES + i * EDGE, EDGES + (i + 1) * EDGE)
            x0[i, 0, at : at + EDGE] = take(even_y, first, second, strip)
            sides = take(even_y, first, second, slice(last, last + 1))
            for j in range(EDGE):
                x0[i, 1, at + j : at + j + 1] = roll_x(sides, -(4 + 8 * (i * EDGE + j)))
        for t in (0, 1):
            x0[i, t, HALO0 : HALO0 + rows] = keep0[6 + i, t, HALO0 : HALO0 + rows]
    for t in (0, 1):
        for row in range(-2, rows // 2 + 2):
            at = row // 2 - LO_UP + 1
            value = spread_x(yu[t, at : at + 1], 1, row & 1)
            for i, fine in enumerate((jnp.where(even, value, roll_z(value, 1)), jnp.where(even, roll_z(value, -1), value))):
                for y in (2 * row, 2 * row + 1):
                    if -EDGE <= y < rows + EDGE:
                        x0[i, t, y + HALO0 : y + HALO0 + 1] = x0[i, t, y + HALO0 : y + HALO0 + 1] + fine
    total = rows + 2 * HALO0
    rows_loop(2, total - 2, lambda r, n: cheb_step(0, keep0, x0, y0, d0, r, n, None, g0))
    rows_loop(3, total - 3, lambda r, n: cheb_step(0, keep0, y0, x0, d0, r, n, CARRY1, g1))
    rows_loop(4, total - 4, lambda r, n: cheb_step(0, keep0, x0, y0, d0, r, n, CARRY2, g2))
    for i in (0, 1):
        for y in range(rows):
            out[pl.ds(i * Z * rows + y, Z, stride=rows), :] = y0[i, 0, HALO0 + y]


def call(kernel, out_shapes, scratch, *args, space=pltpu.VMEM):
    out = [jax.ShapeDtypeStruct(shape, jnp.float32) for shape in out_shapes]
    return pl.pallas_call(
        kernel,
        out_shape=out,
        in_specs=[pl.BlockSpec(memory_space=space)] * len(args),
        out_specs=[pl.BlockSpec(memory_space=pltpu.VMEM)] * len(out),
        scratch_shapes=[pltpu.VMEM(s, jnp.float32) if isinstance(s, tuple) else s for s in scratch],
        compiler_params=pltpu.CompilerParams(vmem_limit_bytes=24 * 2**20),
    )(*args)


def swap(value, axis, step):
    count = lax.axis_size(axis)
    assert count % 2 == 0
    pairs = [(i, (i + step) % count) for i in range(0, count, 2)]
    return lax.ppermute(value, axis, pairs + [(j, i) for i, j in pairs])


def exchange(first, second, axis):
    return swap(first, axis, -1), swap(second, axis, 1)


def body(state, previous, feed, kill):
    _, depth, rows, cols = state.shape
    assert depth == Z and cols == X and rows == 4 * OWN
    across, count = lax.axis_size("gx"), lax.axis_size("gy")
    total0 = rows + 2 * HALO0
    state = state.reshape(2 * Z * rows, X)
    previous = previous.reshape(2 * Z * rows, X)
    feed = feed.reshape(Z * rows, X)
    kill = kill.reshape(Z * rows, X)
    inputs = (state, previous, feed, kill)

    strip = (FIELDS1 + 2 * OWN, Z, X)
    first, second, main, coarse, packet = call(
        functools.partial(first_kernel, rows),
        [strip, strip, (6, rows, Z, X), (2 * OWN, Z, X), (2 * across * count, Z, X)],
        [*(a.shape for a in inputs), pltpu.SemaphoreType.DMA((4,))],
        *(pltpu.with_memory_space_constraint(a, pltpu.HBM) for a in inputs),
        space=pltpu.HBM,
    )
    fields2 = lax.all_to_all(packet, ("gx", "gy"), 0, 0, tiled=True)
    y_packets = exchange(first, second, "gy")

    entries = 6 * total0 + 2 * GROUPS1
    assert entries % PER == 0
    strip = (entries // PER, Z, X)
    first, second = call(
        functools.partial(pack_x_kernel, rows), [strip, strip], [(entries, Z, X)], main, coarse, *y_packets
    )
    x_packets = exchange(first, second, "gx")

    strip = (EDGES + 2 * EDGE + 1, Z, X)
    pair0 = (2, 2, total0, Z, X)
    own, first, second, keep0, gain = call(
        functools.partial(level0_kernel, rows),
        [(2, OWN, Z, X), strip, strip, (8, 2, total0, Z, X), (9, Z, X)],
        [(6, 2, total0, Z, X), pair0, pair0, pair0],
        main,
        *y_packets,
        *x_packets,
        fields2,
    )
    coef1, coef2 = call(
        functools.partial(coarse_kernel, across, count, rows),
        [(3, 2, SIZE1, Z, X), (2, 2, SIZE2, Z, X)],
        [(2, 2 * GROUPS1, Z, X)],
        coarse,
        *y_packets,
        *x_packets,
        fields2,
        gain,
    )
    b_packets = exchange(first, second, "gy")

    one, two, up = (2, SIZE1, Z, X), (2, SIZE2, Z, X), (2, SIZE_UP, Z, X)
    packet, keep1 = call(
        level1_kernel, [(across * count, Z, X), (2, *one)], [one, one], own, *b_packets, coef1, gain
    )
    gathered = lax.all_to_all(packet, ("gx", "gy"), 0, 0, tiled=True)

    (out,) = call(
        functools.partial(rest_kernel, across, count),
        [(2 * Z * rows, X)],
        [one, two, two, two, two, up, up, pair0, pair0, pair0],
        gathered,
        gain,
        coef1,
        coef2,
        keep0,
        keep1,
        *b_packets,
    )
    return out.reshape(2, Z, rows, X)


def solution(mesh):
    placed = (
        P(None, None, "gy", "gx"),
        P(None, None, "gy", "gx"),
        P(None, "gy", "gx"),
        P(None, "gy", "gx"),
    )
    return jax.shard_map(
        body, mesh=mesh, in_specs=placed, out_specs=P(None, None, "gy", "gx"), check_vma=False
    )
```

profile of v0, /device:TPU:0, one launch (start us, length us, event | category | flops | bytes accessed | tf_op | source)
XLA Modules:
  0.0 52.5 jit_solution(7700208820826416095)
XLA Ops:
  0.0 2.2 %shard_map.46 = (f32[32,8,128]{2,1,0:T(8,128)S(1)}, f32[32,8,128]{2,1,0:T(8,128)S(1)}, f32[6,16,8,128]{3,2,1,0:T(8,128)S(1)}, f32[8,8,128]{2,1,0:T(8,128)S(1)}, f32[64,8,128]{2,1,0:T(8,128)}) custom-call(f32[256,128]{1,0:T(8,128)} %bitcast.5, f32[256,128]{1,0:T(8,128)} %bitcast.6, f32[128,128]{1,0:T(8,128)} %bitcast.7, f32[128,128]{1,0:T(8,128)} %bitcast.8), custom_call_target="tpu_custom_call" | custom-call | tf_op jit(solution)/shard_map/pallas_call | solution.py:570
  2.2 7.3 %all-to-all-start = ((f32[64,8,128]{2,1,0:T(8,128)}), f32[64,8,128]{2,1,0:T(8,128)S(1)}, u32[]{:S(2)}, u32[]{:S(2)}) async-start(f32[64,8,128]{2,1,0:T(8,128)} %get-tuple-element.27), calls=%async_computation | async-start | bytes 524288 | tf_op jit(solution)/shard_map/all_to_all | solution.py:610
  9.5 4.6 %collective-permute-start = (f32[32,8,128]{2,1,0:T(8,128)S(1)}, f32[32,8,128]{2,1,0:T(8,128)S(1)}, u32[]{:S(2)}, u32[]{:S(2)}) collective-permute-start(f32[32,8,128]{2,1,0:T(8,128)S(1)} %get-tuple-element.22), channel_id=1, source_target_pairs={{0,7},{2,1},{4,3},{6,5},{7,0},{1,2},{3,4},{5,6},{8,15},{10,9},{12,... | collective-permute-start | bytes 393224 | tf_op jit(solution)/shard_map/ppermute | solution.py:584
  14.1 0.0 collective-permute-start.1
  14.1 8.2 %collective-permute-done.y_first = f32[32,8,128]{2,1,0:T(8,128)S(1)} collective-permute-done((f32[32,8,128]{2,1,0:T(8,128)S(1)}, f32[32,8,128]{2,1,0:T(8,128)S(1)}, u32[]{:S(2)}, u32[]{:S(2)}) %collective-permute-start) | collective-permute-done | bytes 131104 | tf_op jit(solution)/shard_map/ppermute | solution.py:584
  22.3 0.6 %collective-permute-done.1.y_second = f32[32,8,128]{2,1,0:T(8,128)S(1)} collective-permute-done((f32[32,8,128]{2,1,0:T(8,128)S(1)}, f32[32,8,128]{2,1,0:T(8,128)S(1)}, u32[]{:S(2)}, u32[]{:S(2)}) %collective-permute-start.1) | collective-permute-done | bytes 131104 | tf_op jit(solution)/shard_map/ppermute | solution.py:584
  22.9 0.4 shard_map.47
  23.3 0.1 collective-permute-start.2
  23.4 1.4 %collective-permute-start.3 = (f32[24,8,128]{2,1,0:T(8,128)S(1)}, f32[24,8,128]{2,1,0:T(8,128)S(1)}, u32[]{:S(2)}, u32[]{:S(2)}) collective-permute-start(f32[24,8,128]{2,1,0:T(8,128)S(1)} %get-tuple-element.26), channel_id=1, source_target_pairs={{0,8},{16,24},{8,0},{24,16},{1,9},{17,25},{9,1},{25,17},{2,10},{18... | collective-permute-start | bytes 294920 | tf_op jit(solution)/shard_map/ppermute | solution.py:584
  24.8 3.5 %collective-permute-done.2.x_first = f32[24,8,128]{2,1,0:T(8,128)S(1)} collective-permute-done((f32[24,8,128]{2,1,0:T(8,128)S(1)}, f32[24,8,128]{2,1,0:T(8,128)S(1)}, u32[]{:S(2)}, u32[]{:S(2)}) %collective-permute-start.2) | collective-permute-done | bytes 98336 | tf_op jit(solution)/shard_map/ppermute | solution.py:584
  28.4 0.0 collective-permute-done.3.x_second
  28.4 0.0 all-to-all-done.gathered
  28.4 3.0 %shard_map.48 = (f32[2,4,8,128]{3,2,1,0:T(8,128)S(1)}, f32[12,8,128]{2,1,0:T(8,128)S(1)}, f32[12,8,128]{2,1,0:T(8,128)S(1)}, f32[8,2,24,8,128]{4,3,2,1,0:T(8,128)S(1)}, f32[9,8,128]{2,1,0:T(8,128)S(1)}) custom-call(f32[6,16,8,128]{3,2,1,0:T(8,128)S(1)} %get-tuple-element.21.main, f32[32,8,128]{2,1,0:T(8,128)S(1)} %collective-permute-done.y_first, ...), custom_call_target="tpu_custom_call" | custom-call | tf_op jit(solution)/shard_map/pallas_call | solution.py:570
  31.4 1.4 %collective-permute-start.4 = (f32[12,8,128]{2,1,0:T(8,128)S(1)}, f32[12,8,128]{2,1,0:T(8,128)S(1)}, u32[]{:S(2)}, u32[]{:S(2)}) collective-permute-start(f32[12,8,128]{2,1,0:T(8,128)S(1)} %get-tuple-element.29), channel_id=1, source_target_pairs={{0,7},{2,1},{4,3},{6,5},{7,0},{1,2},{3,4},{5,6},{8,15},{10,9},{12,... | collective-permute-start | bytes 147464 | tf_op jit(solution)/shard_map/ppermute | solution.py:584
  32.8 0.0 collective-permute-start.5
  32.8 0.2 shard_map.49
  32.9 5.3 %collective-permute-done.4.first = f32[12,8,128]{2,1,0:T(8,128)S(1)} collective-permute-done((f32[12,8,128]{2,1,0:T(8,128)S(1)}, f32[12,8,128]{2,1,0:T(8,128)S(1)}, u32[]{:S(2)}, u32[]{:S(2)}) %collective-permute-start.4) | collective-permute-done | bytes 49184 | tf_op jit(solution)/shard_map/ppermute | solution.py:584
  38.2 0.0 collective-permute-done.5.second
  38.2 0.6 %shard_map.50 = (f32[32,8,128]{2,1,0:T(8,128)S(1)}, f32[2,2,14,8,128]{4,3,2,1,0:T(8,128)S(1)}) custom-call(f32[2,4,8,128]{3,2,1,0:T(8,128)S(1)} %get-tuple-element.28.own, f32[12,8,128]{2,1,0:T(8,128)S(1)} %collective-permute-done.4.first, f32[12,8,128]{2,1,0:T(8,128)S(1)} %collective-permute-done.5.second, ...), custom_call_target="tpu_custom_call" | custom-call | tf_op jit(solution)/shard_map/pallas_call | solution.py:570
  38.8 10.1 %all_to_all.10.gathered = f32[32,8,128]{2,1,0:T(8,128)S(1)} all-to-all(f32[32,8,128]{2,1,0:T(8,128)S(1)} %get-tuple-element.33), channel_id=1, replica_groups=mesh['gx'=4,'gy'=8] {'gx','gy'}, dimensions={0} | all-to-all | bytes 262144 | tf_op jit(solution)/shard_map/all_to_all | solution.py:648
  48.9 3.7 %shard_map.51 = f32[256,128]{1,0:T(8,128)} custom-call(f32[32,8,128]{2,1,0:T(8,128)S(1)} %all_to_all.10.gathered, f32[9,8,128]{2,1,0:T(8,128)S(1)} %get-tuple-element.31.gain, f32[3,2,14,8,128]{4,3,2,1,0:T(8,128)S(1)} %get-tuple-element.32.coef1, f32[2,2,7,8,128]{4,3,2,1,0:T(8,128)S(1)} %get-tuple-element.34.coef2, ...), custom_call_target="tpu_custom_call" | custom-call | tf_op jit(solution)/shard_map/pallas_call | solution.py:570
Async XLA Ops:
  2.2 26.2 %all-to-all-start = ((f32[64,8,128]{2,1,0:T(8,128)}), f32[64,8,128]{2,1,0:T(8,128)S(1)}, u32[]{:S(2)}, u32[]{:S(2)}) async-start(f32[64,8,128]{2,1,0:T(8,128)} %get-tuple-element.27), calls=%async_computation | async-start | bytes 524288 | tf_op jit(solution)/shard_map/all_to_all | solution.py:610
  9.5 12.8 %collective-permute-start = (f32[32,8,128]{2,1,0:T(8,128)S(1)}, f32[32,8,128]{2,1,0:T(8,128)S(1)}, u32[]{:S(2)}, u32[]{:S(2)}) collective-permute-start(f32[32,8,128]{2,1,0:T(8,128)S(1)} %get-tuple-element.22), channel_id=1, source_target_pairs={{0,7},{2,1},{4,3},{6,5},{7,0},{1,2},{3,4},{5,6},{8,15},{10,9},{12,... | collective-permute-start | bytes 393224 | tf_op jit(solution)/shard_map/ppermute | solution.py:584
  14.1 8.8 %collective-permute-start.1 = (f32[32,8,128]{2,1,0:T(8,128)S(1)}, f32[32,8,128]{2,1,0:T(8,128)S(1)}, u32[]{:S(2)}, u32[]{:S(2)}) collective-permute-start(f32[32,8,128]{2,1,0:T(8,128)S(1)} %get-tuple-element.23), channel_id=1, source_target_pairs={{0,1},{2,3},{4,5},{6,7},{1,0},{3,2},{5,4},{7,6},{8,9},{10,11},{12,... | collective-permute-start | bytes 393224 | tf_op jit(solution)/shard_map/ppermute | solution.py:584
  23.3 5.0 %collective-permute-start.2 = (f32[24,8,128]{2,1,0:T(8,128)S(1)}, f32[24,8,128]{2,1,0:T(8,128)S(1)}, u32[]{:S(2)}, u32[]{:S(2)}) collective-permute-start(f32[24,8,128]{2,1,0:T(8,128)S(1)} %get-tuple-element.25), channel_id=1, source_target_pairs={{0,24},{16,8},{24,0},{8,16},{1,25},{17,9},{25,1},{9,17},{2,26},{18... | collective-permute-start | bytes 294920 | tf_op jit(solution)/shard_map/ppermute | solution.py:584
  23.4 5.0 %collective-permute-start.3 = (f32[24,8,128]{2,1,0:T(8,128)S(1)}, f32[24,8,128]{2,1,0:T(8,128)S(1)}, u32[]{:S(2)}, u32[]{:S(2)}) collective-permute-start(f32[24,8,128]{2,1,0:T(8,128)S(1)} %get-tuple-element.26), channel_id=1, source_target_pairs={{0,8},{16,24},{8,0},{24,16},{1,9},{17,25},{9,1},{25,17},{2,10},{18... | collective-permute-start | bytes 294920 | tf_op jit(solution)/shard_map/ppermute | solution.py:584
  31.4 6.8 %collective-permute-start.4 = (f32[12,8,128]{2,1,0:T(8,128)S(1)}, f32[12,8,128]{2,1,0:T(8,128)S(1)}, u32[]{:S(2)}, u32[]{:S(2)}) collective-permute-start(f32[12,8,128]{2,1,0:T(8,128)S(1)} %get-tuple-element.29), channel_id=1, source_target_pairs={{0,7},{2,1},{4,3},{6,5},{7,0},{1,2},{3,4},{5,6},{8,15},{10,9},{12,... | collective-permute-start | bytes 147464 | tf_op jit(solution)/shard_map/ppermute | solution.py:584
  32.8 5.4 %collective-permute-start.5 = (f32[12,8,128]{2,1,0:T(8,128)S(1)}, f32[12,8,128]{2,1,0:T(8,128)S(1)}, u32[]{:S(2)}, u32[]{:S(2)}) collective-permute-start(f32[12,8,128]{2,1,0:T(8,128)S(1)} %get-tuple-element.30), channel_id=1, source_target_pairs={{0,1},{2,3},{4,5},{6,7},{1,0},{3,2},{5,4},{7,6},{8,9},{10,11},{12,... | collective-permute-start | bytes 147464 | tf_op jit(solution)/shard_map/ppermute | solution.py:584
where the time goes:
time: 52.8 us; the launch traced here: 52.5 us
  waiting for transfers between devices  17.6 us (33%)
  starting transfers between devices  14.8 us (28%)
  blocking collectives  10.1 us (19%)
  Pallas kernels  10 us (19%)
    ppermute x6, waiting for transfers between devices, swap(): return lax.ppermute(value, axis, pairs + [(j, i) for i, j in pairs])  17.6 us
    all_to_all x1, blocking collectives, body(): gathered = lax.all_to_all(packet, ('gx', 'gy'), 0, 0, tiled=True)  10.1 us
    pallas_call x6, Pallas kernels, call(): pl.pallas_call(kernel, out_shape=out, in_specs=[pl.BlockSpec(memory_space...  10 us
    ppermute x6, starting transfers between devices, swap(): return lax.ppermute(value, axis, pairs + [(j, i) for i, j in pairs])  7.47 us
    all_to_all x1, starting transfers between devices, body(): fields2 = lax.all_to_all(packet, ('gx', 'gy'), 0, 0, tiled=True)  7.3 us
  transfers between devices with their start and end apart: 7, of which 4 were waited for; matrix products, arithmetic and copies ran while one was open for 0% of the time, Pallas kernels for 1%

commit v1 on v0

--- a/solution.py
+++ b/solution.py
@@ -21,8 +21,13 @@
 Z = 8
 X = 128
 HALO0 = 4
+HALOS = (4, 4, 3, 3, 3, 3)
+STARTS = tuple(sum(HALOS[:i]) for i in range(6))
+FIELDS1 = sum(HALOS)
+FIELDS2 = FIELDS1 + 8
 WIDE = 18
 PER = X // WIDE
+WIDE2 = 32
 EDGE = 3
 CHUNK = 4
 
@@ -134,9 +139,9 @@
 
 
 def write_gains(spread, out):
-    row = lax.broadcasted_iota(jnp.int32, (Z, X), 0)
+    lane = lax.broadcasted_iota(jnp.int32, (1, X), 1)
     for level in range(3):
-        top = jnp.max(jnp.where(row == level, spread, 0.0), axis=0, keepdims=True)
+        top = jnp.max(jnp.where(lane == level, spread, 0.0), axis=1, keepdims=True)
         tau = 1.0 / (1.0 + jnp.broadcast_to(top, (Z, X)))
         for i, factor in enumerate((1.0 / _CENTRE, 2.0 * _RHO1 / _HALF, 2.0 * _RHO2 / _HALF)):
             out[3 * level + i] = factor * tau
@@ -244,9 +249,6 @@
     return ref[pl.ds(f * Z * rows + y, Z, stride=rows), :]
 
 
-FIELDS1 = 6 * HALO0
-
-
 def is_even(axis):
     return lax.rem(lax.axis_index(axis), 2) == 0
 
@@ -259,7 +261,7 @@
     return jnp.where(even, second[at], first[at])
 
 
-def first_kernel(rows, state, previous, feed, kill, first, second, main, coarse, packet, *scratch):
+def first_kernel(rows, state, previous, feed, kill, first, second, main, coarse, *scratch):
     sources, sems = scratch[:4], scratch[4]
     copies = [
         pltpu.make_async_copy(ref, held, sems.at[i])
@@ -275,8 +277,8 @@
     for i, (ref, f) in enumerate(fields):
         for y in range(rows):
             main[i, y] = plane(ref, f, y, rows)
-        top, bottom = main[i, 0:HALO0], main[i, rows - HALO0 : rows]
-        at = slice(i * HALO0, (i + 1) * HALO0)
+        top, bottom = main[i, 0 : HALOS[i]], main[i, rows - HALOS[i] : rows]
+        at = slice(STARTS[i], STARTS[i] + HALOS[i])
         first[at] = jnp.where(even, top, bottom)
         second[at] = jnp.where(even, bottom, top)
     u, v, f, k = (main[i] for i in (0, 1, 4, 5))
@@ -291,30 +293,40 @@
         for ref in (first, second):
             ref[FIELDS1 + p * OWN : FIELDS1 + (p + 1) * OWN] = pairs[p]
 
-    row = lax.broadcasted_iota(jnp.int32, (Z, X), 0)
+    uv, fk = (restrict_12([pair[j : j + 1] for j in range(OWN)]) for pair in pairs)
+    both = jnp.where((sub_of() & 2) == 0, uv, fk)
+    coarse[2 * OWN : 2 * OWN + 1] = both
+    for ref in (first, second):
+        ref[FIELDS2 : FIELDS2 + 1] = both
+
+
+def split_fields2(both):
+    low = (sub_of() & 2) == 0
+    return jnp.where(low, both, roll_z(both, 2)), jnp.where(low, roll_z(both, -2), both)
+
+
+def spread_kernel(main, coarse, out):
+    lane = lax.broadcasted_iota(jnp.int32, (1, X), 1)
+    u, v, f, k = (main[i] for i in (0, 1, 4, 5))
     cross, squared, inv_u, inv_v, _, _ = jacobian(u, v, f, k, 0)
     tops = [jnp.max(jnp.maximum((6.0 * DIFF[0] + cross) * inv_u, (6.0 * DIFF[1] + squared) * inv_v), axis=0)]
-    tops.append(jnp.max(packed_spread(*pairs, 1), axis=0))
-    uv, fk = (restrict_12([pair[j : j + 1] for j in range(OWN)]) for pair in pairs)
-    tops.append(packed_spread(uv, fk, 2)[0])
-    both = jnp.where((sub_of() & 2) == 0, uv, fk)[0]
-    result = jnp.zeros((Z, X), jnp.float32)
+    tops.append(jnp.max(packed_spread(coarse[0:OWN], coarse[OWN : 2 * OWN], 1), axis=0))
+    tops.append(packed_spread(*split_fields2(coarse[2 * OWN : 2 * OWN + 1]), 2)[0])
+    result = jnp.zeros((1, X), jnp.float32)
     for level, top in enumerate(tops):
-        top = jnp.max(jnp.max(top, axis=1, keepdims=True), axis=0, keepdims=True)
-        result = jnp.where(row == level, jnp.broadcast_to(top, (Z, X)), result)
-    for c in range(packet.shape[0] // 2):
-        packet[2 * c] = both
-        packet[2 * c + 1] = result
-
-
-def around(across, count, gathered, chunk):
+        top = jnp.max(jnp.max(top, axis=0, keepdims=True), axis=1, keepdims=True)
+        result = jnp.where(lane == level, jnp.broadcast_to(top, (1, X)), result)
+    out[...] = jnp.broadcast_to(result[None], out.shape)
+
+
+def around(across, count, gathered):
     lane = lane_of()
     gx, gy = lax.axis_index("gx"), lax.axis_index("gy")
     columns = [lax.rem(gx + i + across, across) * count for i in (-1, 0, 1)]
     out = [[], []]
     for q in range(LO2, HI2):
         row = lax.rem(gy + q + 4 * count, count)
-        left, centre, right = (gathered[pl.ds((column + row) * chunk, 1)] for column in columns)
+        left, centre, right = (gathered[pl.ds(column + row, 1)] for column in columns)
         out[0].append(centre)
         out[1].append(jnp.where(lane < X // 2, right, left))
     return [jnp.concatenate(groups, axis=0) for groups in out]
@@ -322,6 +334,17 @@
 
 GROUPS1 = HI1 - LO1
 GROUPS2 = HI2 - LO2
+
+
+def entry(rows, i):
+    starts = [0]
+    for halo in HALOS:
+        starts.append(starts[-1] + rows + 2 * halo)
+    return (starts + [starts[-1] + 2 * GROUPS1])[i]
+
+
+def entry_tiles(rows):
+    return -(-entry(rows, 7) // PER)
 
 
 def pack_slots(parts, width):
@@ -338,29 +361,53 @@
     return jnp.where(lane_of() < X // 2, roll_x(from_right, -width * j), roll_x(from_left, X - width - width * j))
 
 
+def unpack_entries(even_x, x_first, x_second, share, lo, hi):
+    out = []
+    for j in range(PER):
+        a, b = max(lo, j * share), min(hi, (j + 1) * share)
+        if a < b:
+            strip = slice(a - j * share, b - j * share)
+            left, right = prev_of(even_x, x_first, x_second, strip), next_of(even_x, x_first, x_second, strip)
+            out.append((a - lo, b - lo, unpack_slot(left, right, j, WIDE)))
+    return out
+
+
+def unpack_fields2(even_x, x_first, x_second, share, j):
+    strip = slice(share, share + 1)
+    left, right = prev_of(even_x, x_first, x_second, strip), next_of(even_x, x_first, x_second, strip)
+    return unpack_slot(left, right, j, WIDE2)
+
+
 def pack_x_kernel(rows, main, coarse, y_first, y_second, first, second, held):
     even = is_even("gy")
-    total = rows + 2 * HALO0
-    share = held.shape[0] // PER
-    for i in range(6):
-        strip = slice(i * HALO0, (i + 1) * HALO0)
-        held[i * total : i * total + HALO0] = prev_of(even, y_first, y_second, strip)
-        held[i * total + HALO0 : i * total + HALO0 + rows] = main[i]
-        held[i * total + HALO0 + rows : (i + 1) * total] = next_of(even, y_first, y_second, strip)
+    share = entry_tiles(rows)
+    for i, halo in enumerate(HALOS):
+        strip = slice(STARTS[i], STARTS[i] + halo)
+        to = entry(rows, i)
+        held[to : to + halo] = prev_of(even, y_first, y_second, strip)
+        held[to + halo : to + halo + rows] = main[i]
+        held[to + halo + rows : to + 2 * halo + rows] = next_of(even, y_first, y_second, strip)
     for p in (0, 1):
-        to = 6 * total + p * GROUPS1
+        to = entry(rows, 6) + p * GROUPS1
         strip = slice(FIELDS1 + p * OWN, FIELDS1 + (p + 1) * OWN)
         held[to : to + OWN] = prev_of(even, y_first, y_second, strip)
         held[to + OWN : to + 2 * OWN] = coarse[p * OWN : (p + 1) * OWN]
         held[to + 2 * OWN : to + 3 * OWN] = next_of(even, y_first, y_second, strip)
     left, right = pack_slots([held[j * share : (j + 1) * share] for j in range(PER)], WIDE)
+    strip = slice(FIELDS2, FIELDS2 + 1)
+    own = coarse[2 * OWN : 2 * OWN + 1]
+    parts = [prev_of(even, y_first, y_second, strip), own, next_of(even, y_first, y_second, strip)]
+    left2, right2 = pack_slots(parts, WIDE2)
     even = is_even("gx")
-    first[...] = jnp.where(even, left, right)
-    second[...] = jnp.where(even, right, left)
+    first[0:share] = jnp.where(even, left, right)
+    second[0:share] = jnp.where(even, right, left)
+    first[share : share + 1] = jnp.where(even, left2, right2)
+    second[share : share + 1] = jnp.where(even, right2, left2)
 
 
 HALO1 = X // (2 * OWN)
 EDGES = OWN + 1
+FAR = EDGES + 2 * EDGE + 1
 
 
 def level0_kernel(
@@ -368,23 +415,20 @@
 ):
     even, even_x = is_even("gy"), is_even("gx")
     total = rows + 2 * HALO0
-    share = (6 * total + 2 * GROUPS1) // PER
-    top = gathered[1]
-    for c in range(1, gathered.shape[0] // 2):
-        top = jnp.maximum(top, gathered[2 * c + 1])
+    share = entry_tiles(rows)
+    top = gathered[0]
+    for c in range(1, gathered.shape[0]):
+        top = jnp.maximum(top, gathered[c])
     write_gains(top, gain_out)
     g0, g1, g2 = (gain_out[i] for i in range(3))
-    for i in range(6):
-        strip = slice(i * HALO0, (i + 1) * HALO0)
-        fields[i, 0, 0:HALO0] = prev_of(even, y_first, y_second, strip)
+    for i, halo in enumerate(HALOS):
+        strip = slice(STARTS[i], STARTS[i] + halo)
+        skip = HALO0 - halo
+        fields[i, 0, skip:HALO0] = prev_of(even, y_first, y_second, strip)
         fields[i, 0, HALO0 : HALO0 + rows] = main[i]
-        fields[i, 0, HALO0 + rows : total] = next_of(even, y_first, y_second, strip)
-        for j in range(PER):
-            lo, hi = max(i * total, j * share), min((i + 1) * total, (j + 1) * share)
-            if lo < hi:
-                strip = slice(lo - j * share, hi - j * share)
-                left, right = prev_of(even_x, x_first, x_second, strip), next_of(even_x, x_first, x_second, strip)
-                fields[i, 1, lo - i * total : hi - i * total] = unpack_slot(left, right, j, WIDE)
+        fields[i, 0, HALO0 + rows : total - skip] = next_of(even, y_first, y_second, strip)
+        for a, b, value in unpack_entries(even_x, x_first, x_second, share, entry(rows, i), entry(rows, i + 1)):
+            fields[i, 1, a + skip : b + skip] = value
     here = keep.at[6:8]
 
     def setup(r, n):
@@ -445,37 +489,53 @@
     top, bottom = (jnp.concatenate(parts, axis=0) for parts in edges)
     for ref in (first, second):
         ref[OWN : OWN + 1] = sides
+    strip = slice(FIELDS2, FIELDS2 + 1)
+    for t in (0, 1):
+        if t == 0:
+            before, after = prev_of(even, y_first, y_second, strip), next_of(even, y_first, y_second, strip)
+        else:
+            before, after = (unpack_fields2(even_x, x_first, x_second, share, j) for j in (0, 2))
+        first[FAR + t : FAR + t + 1] = jnp.where(even, after, before)
+        second[FAR + t : FAR + t + 1] = jnp.where(even, before, after)
     first[EDGES : EDGES + 2 * EDGE + 1] = jnp.where(even, top, bottom)
     second[EDGES : EDGES + 2 * EDGE + 1] = jnp.where(even, bottom, top)
 
 
-def coarse_kernel(
-    across, count, rows, coarse, y_first, y_second, x_first, x_second, gathered, gain, coef1, coef2, fields
-):
+def coarse1_kernel(rows, coarse, y_first, y_second, x_first, x_second, gain, coef, fields):
     del gain
     even, even_x = is_even("gy"), is_even("gx")
-    share = (6 * (rows + 2 * HALO0) + 2 * GROUPS1) // PER
-    base = 6 * (rows + 2 * HALO0) - (PER - 1) * share
+    share = entry_tiles(rows)
     for p in (0, 1):
         to = p * GROUPS1
         strip = slice(FIELDS1 + p * OWN, FIELDS1 + (p + 1) * OWN)
         fields[0, to : to + OWN] = prev_of(even, y_first, y_second, strip)
         fields[0, to + OWN : to + 2 * OWN] = coarse[p * OWN : (p + 1) * OWN]
         fields[0, to + 2 * OWN : to + 3 * OWN] = next_of(even, y_first, y_second, strip)
-    strip = slice(base, share)
-    left, right = prev_of(even_x, x_first, x_second, strip), next_of(even_x, x_first, x_second, strip)
-    fields[1] = unpack_slot(left, right, PER - 1, WIDE)
+    for a, b, value in unpack_entries(even_x, x_first, x_second, share, entry(rows, 6), entry(rows, 7)):
+        fields[1, a:b] = value
     for t in (0, 1):
         for i, value in enumerate(packed_jacobian(fields[t, 0:GROUPS1], fields[t, GROUPS1 : 2 * GROUPS1], 1)):
-            coef1[i, t, 1 : SIZE1 - 1] = value
-
-    sub = sub_of()
-    for t, both in enumerate(around(across, count, gathered, 2)):
-        uv = jnp.where((sub & 2) == 0, both, roll_z(both, 2))
-        fk = jnp.where((sub & 2) == 0, roll_z(both, -2), both)
-        inverse, other, _ = packed_jacobian(uv, fk, 2)
-        coef2[0, t, 1 : SIZE2 - 1] = inverse
-        coef2[1, t, 1 : SIZE2 - 1] = other
+            coef[i, t, 1 : SIZE1 - 1] = value
+
+
+def coarse2_kernel(rows, coarse, y_first, y_second, x_first, x_second, b_first, b_second, coef):
+    even, even_x = is_even("gy"), is_even("gx")
+    share = entry_tiles(rows)
+    near = slice(FIELDS2, FIELDS2 + 1)
+    for t in (0, 1):
+        far = slice(FAR + t, FAR + t + 1)
+        if t == 0:
+            middle = [
+                prev_of(even, y_first, y_second, near),
+                coarse[2 * OWN : 2 * OWN + 1],
+                next_of(even, y_first, y_second, near),
+            ]
+        else:
+            middle = [unpack_fields2(even_x, x_first, x_second, share, j) for j in range(3)]
+        parts = [prev_of(even, b_first, b_second, far), *middle, next_of(even, b_first, b_second, far)]
+        inverse, other, _ = packed_jacobian(*split_fields2(jnp.concatenate(parts, axis=0)), 2)
+        coef[0, t, 1 : SIZE2 - 1] = inverse
+        coef[1, t, 1 : SIZE2 - 1] = other
 
 
 def level1_kernel(own, first, second, coef1, gain, packet, keep, y1, d1):
@@ -510,7 +570,7 @@
     even = (sub_of() & 1) == 0
     b1, x1 = keep1.at[0], keep1.at[1]
 
-    for t, groups in enumerate(around(across, count, gathered, 1)):
+    for t, groups in enumerate(around(across, count, gathered)):
         b2[t, 1 : SIZE2 - 1] = groups
 
     n = HI2 - LO2
@@ -599,26 +659,30 @@
     kill = kill.reshape(Z * rows, X)
     inputs = (state, previous, feed, kill)
 
-    strip = (FIELDS1 + 2 * OWN, Z, X)
-    first, second, main, coarse, packet = call(
+    strip = (FIELDS2 + 1, Z, X)
+    first, second, main, coarse = call(
         functools.partial(first_kernel, rows),
-        [strip, strip, (6, rows, Z, X), (2 * OWN, Z, X), (2 * across * count, Z, X)],
+        [strip, strip, (6, rows, Z, X), (2 * OWN + 1, Z, X)],
         [*(a.shape for a in inputs), pltpu.SemaphoreType.DMA((4,))],
         *(pltpu.with_memory_space_constraint(a, pltpu.HBM) for a in inputs),
         space=pltpu.HBM,
     )
-    fields2 = lax.all_to_all(packet, ("gx", "gy"), 0, 0, tiled=True)
     y_packets = exchange(first, second, "gy")
-
-    entries = 6 * total0 + 2 * GROUPS1
-    assert entries % PER == 0
-    strip = (entries // PER, Z, X)
+    (spread,) = call(spread_kernel, [(across * count, 1, X)], [], main, coarse)
+    spread = lax.all_to_all(spread, ("gx", "gy"), 0, 0, tiled=True)
+
+    strip = (entry_tiles(rows) + 1, Z, X)
     first, second = call(
-        functools.partial(pack_x_kernel, rows), [strip, strip], [(entries, Z, X)], main, coarse, *y_packets
+        functools.partial(pack_x_kernel, rows),
+        [strip, strip],
+        [(PER * entry_tiles(rows), Z, X)],
+        main,
+        coarse,
+        *y_packets,
     )
     x_packets = exchange(first, second, "gx")
 
-    strip = (EDGES + 2 * EDGE + 1, Z, X)
+    strip = (FAR + 2, Z, X)
     pair0 = (2, 2, total0, Z, X)
     own, first, second, keep0, gain = call(
         functools.partial(level0_kernel, rows),
@@ -627,16 +691,15 @@
         main,
         *y_packets,
         *x_packets,
-        fields2,
-    )
-    coef1, coef2 = call(
-        functools.partial(coarse_kernel, across, count, rows),
-        [(3, 2, SIZE1, Z, X), (2, 2, SIZE2, Z, X)],
+        spread,
+    )
+    (coef1,) = call(
+        functools.partial(coarse1_kernel, rows),
+        [(3, 2, SIZE1, Z, X)],
         [(2, 2 * GROUPS1, Z, X)],
         coarse,
         *y_packets,
         *x_packets,
-        fields2,
         gain,
     )
     b_packets = exchange(first, second, "gy")
@@ -646,6 +709,15 @@
         level1_kernel, [(across * count, Z, X), (2, *one)], [one, one], own, *b_packets, coef1, gain
     )
     gathered = lax.all_to_all(packet, ("gx", "gy"), 0, 0, tiled=True)
+    (coef2,) = call(
+        functools.partial(coarse2_kernel, rows),
+        [(2, 2, SIZE2, Z, X)],
+        [],
+        coarse,
+        *y_packets,
+        *x_packets,
+        *b_packets,
+    )
 
     (out,) = call(
         functools.partial(rest_kernel, across, count),

time: 52.8 us -> 50.2 us (0.951)
  starting transfers between devices: 14.8 us -> 12.4 us
  blocking collectives: 10.1 us -> 9.18 us
    all_to_all x1, waiting for transfers between devices: 0.01 us -> 7.63 us  [body(): gathered = lax.all_to_all(packet, ('gx', 'gy'), 0, 0, tiled=True)]
    ppermute x6, waiting for transfers between devices: 17.6 us -> 10.5 us  [swap(): return lax.ppermute(value, axis, pairs + [(j, i) for i, j in pairs])]
    all_to_all x1, starting transfers between devices: 7.3 us -> 2.58 us  [body(): gathered = lax.all_to_all(packet, ('gx', 'gy'), 0, 0, tiled=True)]
    ppermute x6, starting transfers between devices: 7.47 us -> 9.8 us  [swap(): return lax.ppermute(value, axis, pairs + [(j, i) for i, j in pairs])]
    all_to_all x1, blocking collectives: 10.1 us -> 9.18 us  [body(): spread = lax.all_to_all(spread, ('gx', 'gy'), 0, 0, tiled=True)]
    pallas_call x6 -> x8, Pallas kernels: 10 us -> 10.2 us  [call(): pl.pallas_call(kernel, out_shape=out, in_specs=[pl.BlockSpec(memory_space...]
where the time goes in v1:
time: 50.2 us; the launch traced here: 49.9 us
  waiting for transfers between devices  18.1 us (36%)
  starting transfers between devices  12.4 us (25%)
  Pallas kernels  10.2 us (20%)
  blocking collectives  9.18 us (18%)
    ppermute x6, waiting for transfers between devices, swap(): return lax.ppermute(value, axis, pairs + [(j, i) for i, j in pairs])  10.5 us
    pallas_call x8, Pallas kernels, call(): pl.pallas_call(kernel, out_shape=out, in_specs=[pl.BlockSpec(memory_space...  10.2 us
    ppermute x6, starting transfers between devices, swap(): return lax.ppermute(value, axis, pairs + [(j, i) for i, j in pairs])  9.8 us
    all_to_all x1, blocking collectives, body(): spread = lax.all_to_all(spread, ('gx', 'gy'), 0, 0, tiled=True)  9.18 us
    all_to_all x1, waiting for transfers between devices, body(): gathered = lax.all_to_all(packet, ('gx', 'gy'), 0, 0, tiled=True)  7.63 us
    all_to_all x1, starting transfers between devices, body(): gathered = lax.all_to_all(packet, ('gx', 'gy'), 0, 0, tiled=True)  2.58 us
  transfers between devices with their start and end apart: 7, of which 4 were waited for; matrix products, arithmetic and copies ran while one was open for 0% of the time, Pallas kernels for 1%

profile of v1, /device:TPU:0, one launch (start us, length us, event | category | flops | bytes accessed | tf_op | source)
XLA Modules:
  0.0 49.9 jit_solution(17282271540042283072)
XLA Ops:
  0.0 1.4 %shard_map.46 = (f32[29,8,128]{2,1,0:T(8,128)S(1)}, f32[29,8,128]{2,1,0:T(8,128)S(1)}, f32[6,16,8,128]{3,2,1,0:T(8,128)S(1)}, f32[9,8,128]{2,1,0:T(8,128)S(1)}) custom-call(f32[256,128]{1,0:T(8,128)} %bitcast.5, f32[256,128]{1,0:T(8,128)} %bitcast.6, f32[128,128]{1,0:T(8,128)} %bitcast.7, f32[128,128]{1,0:T(8,128)} %bitcast.8), custom_call_target="tpu_custom_call" | custom-call | tf_op jit(solution)/shard_map/pallas_call | solution.py:630
  1.4 6.1 %collective-permute-start = (f32[29,8,128]{2,1,0:T(8,128)S(1)}, f32[29,8,128]{2,1,0:T(8,128)S(1)}, u32[]{:S(2)}, u32[]{:S(2)}) collective-permute-start(f32[29,8,128]{2,1,0:T(8,128)S(1)} %get-tuple-element.19), channel_id=1, source_target_pairs={{0,7},{2,1},{4,3},{6,5},{7,0},{1,2},{3,4},{5,6},{8,15},{10,9},{12,... | collective-permute-start | bytes 356360 | tf_op jit(solution)/shard_map/ppermute | solution.py:644
  7.5 0.0 collective-permute-start.1
  7.5 3.3 %collective-permute-done.y_first = f32[29,8,128]{2,1,0:T(8,128)S(1)} collective-permute-done((f32[29,8,128]{2,1,0:T(8,128)S(1)}, f32[29,8,128]{2,1,0:T(8,128)S(1)}, u32[]{:S(2)}, u32[]{:S(2)}) %collective-permute-start) | collective-permute-done | bytes 118816 | tf_op jit(solution)/shard_map/ppermute | solution.py:644
  10.8 2.4 %collective-permute-done.1.y_second = f32[29,8,128]{2,1,0:T(8,128)S(1)} collective-permute-done((f32[29,8,128]{2,1,0:T(8,128)S(1)}, f32[29,8,128]{2,1,0:T(8,128)S(1)}, u32[]{:S(2)}, u32[]{:S(2)}) %collective-permute-start.1) | collective-permute-done | bytes 118816 | tf_op jit(solution)/shard_map/ppermute | solution.py:644
  13.2 0.4 shard_map.47
  13.6 0.9 %collective-permute-start.2 = (f32[24,8,128]{2,1,0:T(8,128)S(1)}, f32[24,8,128]{2,1,0:T(8,128)S(1)}, u32[]{:S(2)}, u32[]{:S(2)}) collective-permute-start(f32[24,8,128]{2,1,0:T(8,128)S(1)} %get-tuple-element.22), channel_id=1, source_target_pairs={{0,24},{16,8},{24,0},{8,16},{1,25},{17,9},{25,1},{9,17},{2,26},{18... | collective-permute-start | bytes 294920 | tf_op jit(solution)/shard_map/ppermute | solution.py:644
  14.6 0.7 %collective-permute-start.3 = (f32[24,8,128]{2,1,0:T(8,128)S(1)}, f32[24,8,128]{2,1,0:T(8,128)S(1)}, u32[]{:S(2)}, u32[]{:S(2)}) collective-permute-start(f32[24,8,128]{2,1,0:T(8,128)S(1)} %get-tuple-element.23), channel_id=1, source_target_pairs={{0,8},{16,24},{8,0},{24,16},{1,9},{17,25},{9,1},{25,17},{2,10},{18... | collective-permute-start | bytes 294920 | tf_op jit(solution)/shard_map/ppermute | solution.py:644
  15.3 0.2 shard_map.48
  15.5 9.2 %all_to_all.10.gathered = f32[32,1,128]{2,1,0:T(1,128)S(1)} all-to-all(f32[32,1,128]{2,1,0:T(1,128)S(1)} %shard_map.48), channel_id=1, replica_groups=mesh['gx'=4,'gy'=8] {'gx','gy'}, dimensions={0} | all-to-all | bytes 32768 | tf_op jit(solution)/shard_map/all_to_all | solution.py:672
  24.7 0.0 collective-permute-done.2.x_first
  24.7 0.0 collective-permute-done.3.x_second
  24.7 3.1 %shard_map.49 = (f32[2,4,8,128]{3,2,1,0:T(8,128)S(1)}, f32[14,8,128]{2,1,0:T(8,128)S(1)}, f32[14,8,128]{2,1,0:T(8,128)S(1)}, f32[8,2,24,8,128]{4,3,2,1,0:T(8,128)S(1)}, f32[9,8,128]{2,1,0:T(8,128)S(1)}) custom-call(f32[6,16,8,128]{3,2,1,0:T(8,128)S(1)} %get-tuple-element.18.main, f32[29,8,128]{2,1,0:T(8,128)S(1)} %collective-permute-done.y_first, ...), custom_call_target="tpu_custom_call" | custom-call | tf_op jit(solution)/shard_map/pallas_call | solution.py:630
  27.8 0.7 %collective-permute-start.4 = (f32[14,8,128]{2,1,0:T(8,128)S(1)}, f32[14,8,128]{2,1,0:T(8,128)S(1)}, u32[]{:S(2)}, u32[]{:S(2)}) collective-permute-start(f32[14,8,128]{2,1,0:T(8,128)S(1)} %get-tuple-element.25), channel_id=1, source_target_pairs={{0,7},{2,1},{4,3},{6,5},{7,0},{1,2},{3,4},{5,6},{8,15},{10,9},{12,... | collective-permute-start | bytes 172040 | tf_op jit(solution)/shard_map/ppermute | solution.py:644
  28.5 1.4 %collective-permute-start.5 = (f32[14,8,128]{2,1,0:T(8,128)S(1)}, f32[14,8,128]{2,1,0:T(8,128)S(1)}, u32[]{:S(2)}, u32[]{:S(2)}) collective-permute-start(f32[14,8,128]{2,1,0:T(8,128)S(1)} %get-tuple-element.26), channel_id=1, source_target_pairs={{0,1},{2,3},{4,5},{6,7},{1,0},{3,2},{5,4},{7,6},{8,9},{10,11},{12,... | collective-permute-start | bytes 172040 | tf_op jit(solution)/shard_map/ppermute | solution.py:644
  29.8 0.2 shard_map.50.coef1
  30.0 4.7 %collective-permute-done.4.first.b_first = f32[14,8,128]{2,1,0:T(8,128)S(1)} collective-permute-done((f32[14,8,128]{2,1,0:T(8,128)S(1)}, f32[14,8,128]{2,1,0:T(8,128)S(1)}, u32[]{:S(2)}, u32[]{:S(2)}) %collective-permute-start.4) | collective-permute-done | bytes 57376 | tf_op jit(solution)/shard_map/ppermute | solution.py:644
  34.7 0.0 collective-permute-done.5.second.b_second
  34.7 1.2 %shard_map.51 = (f32[32,8,128]{2,1,0:T(8,128)}, f32[2,2,14,8,128]{4,3,2,1,0:T(8,128)S(1)}) custom-call(f32[2,4,8,128]{3,2,1,0:T(8,128)S(1)} %get-tuple-element.24.own, f32[14,8,128]{2,1,0:T(8,128)S(1)} %collective-permute-done.4.first.b_first, f32[14,8,128]{2,1,0:T(8,128)S(1)} %collective-permute-done.5.second.b_second, ...), custom_call_target="tpu_custom_call" | custom-call | tf_op jit(solution)/shard_map/pallas_call | solution.py:630
  35.9 2.6 %all-to-all-start.1 = ((f32[32,8,128]{2,1,0:T(8,128)}), f32[32,8,128]{2,1,0:T(8,128)S(1)}, u32[]{:S(2)}, u32[]{:S(2)}) async-start(f32[32,8,128]{2,1,0:T(8,128)} %get-tuple-element.28), calls=%async_computation.1 | async-start | bytes 262144 | tf_op jit(solution)/shard_map/all_to_all | solution.py:711
  38.5 0.1 shard_map.52.coef2
  38.6 7.6 %all-to-all-done.1.gathered = f32[32,8,128]{2,1,0:T(8,128)S(1)} async-done(((f32[32,8,128]{2,1,0:T(8,128)}), f32[32,8,128]{2,1,0:T(8,128)S(1)}, u32[]{:S(2)}, u32[]{:S(2)}) %all-to-all-start.1) | async-done | bytes 131104 | tf_op jit(solution)/shard_map/all_to_all | solution.py:711
  46.3 3.7 %shard_map.53 = f32[256,128]{1,0:T(8,128)} custom-call(f32[32,8,128]{2,1,0:T(8,128)S(1)} %all-to-all-done.1.gathered, f32[9,8,128]{2,1,0:T(8,128)S(1)} %get-tuple-element.27.gain, f32[3,2,14,8,128]{4,3,2,1,0:T(8,128)S(1)} %shard_map.50.coef1, f32[2,2,7,8,128]{4,3,2,1,0:T(8,128)S(1)} %shard_map.52.coef2, f32[8,2,24,8,128]{4,3,2,1,0:T(8,128)S(1)} %get-tuple-element.29.keep0, ...), custom_call_target="tpu_custom_call" | custom-call | tf_op jit(solution)/shard_map/pallas_call | solution.py:630
Async XLA Ops:
  1.4 9.4 %collective-permute-start = (f32[29,8,128]{2,1,0:T(8,128)S(1)}, f32[29,8,128]{2,1,0:T(8,128)S(1)}, u32[]{:S(2)}, u32[]{:S(2)}) collective-permute-start(f32[29,8,128]{2,1,0:T(8,128)S(1)} %get-tuple-element.19), channel_id=1, source_target_pairs={{0,7},{2,1},{4,3},{6,5},{7,0},{1,2},{3,4},{5,6},{8,15},{10,9},{12,... | collective-permute-start | bytes 356360 | tf_op jit(solution)/shard_map/ppermute | solution.py:644
  7.5 5.8 %collective-permute-start.1 = (f32[29,8,128]{2,1,0:T(8,128)S(1)}, f32[29,8,128]{2,1,0:T(8,128)S(1)}, u32[]{:S(2)}, u32[]{:S(2)}) collective-permute-start(f32[29,8,128]{2,1,0:T(8,128)S(1)} %get-tuple-element.20), channel_id=1, source_target_pairs={{0,1},{2,3},{4,5},{6,7},{1,0},{3,2},{5,4},{7,6},{8,9},{10,11},{12,... | collective-permute-start | bytes 356360 | tf_op jit(solution)/shard_map/ppermute | solution.py:644
  13.6 11.0 %collective-permute-start.2 = (f32[24,8,128]{2,1,0:T(8,128)S(1)}, f32[24,8,128]{2,1,0:T(8,128)S(1)}, u32[]{:S(2)}, u32[]{:S(2)}) collective-permute-start(f32[24,8,128]{2,1,0:T(8,128)S(1)} %get-tuple-element.22), channel_id=1, source_target_pairs={{0,24},{16,8},{24,0},{8,16},{1,25},{17,9},{25,1},{9,17},{2,26},{18... | collective-permute-start | bytes 294920 | tf_op jit(solution)/shard_map/ppermute | solution.py:644
  14.6 10.1 %collective-permute-start.3 = (f32[24,8,128]{2,1,0:T(8,128)S(1)}, f32[24,8,128]{2,1,0:T(8,128)S(1)}, u32[]{:S(2)}, u32[]{:S(2)}) collective-permute-start(f32[24,8,128]{2,1,0:T(8,128)S(1)} %get-tuple-element.23), channel_id=1, source_target_pairs={{0,8},{16,24},{8,0},{24,16},{1,9},{17,25},{9,1},{25,17},{2,10},{18... | collective-permute-start | bytes 294920 | tf_op jit(solution)/shard_map/ppermute | solution.py:644
  27.8 6.9 %collective-permute-start.4 = (f32[14,8,128]{2,1,0:T(8,128)S(1)}, f32[14,8,128]{2,1,0:T(8,128)S(1)}, u32[]{:S(2)}, u32[]{:S(2)}) collective-permute-start(f32[14,8,128]{2,1,0:T(8,128)S(1)} %get-tuple-element.25), channel_id=1, source_target_pairs={{0,7},{2,1},{4,3},{6,5},{7,0},{1,2},{3,4},{5,6},{8,15},{10,9},{12,... | collective-permute-start | bytes 172040 | tf_op jit(solution)/shard_map/ppermute | solution.py:644
  28.5 6.2 %collective-permute-start.5 = (f32[14,8,128]{2,1,0:T(8,128)S(1)}, f32[14,8,128]{2,1,0:T(8,128)S(1)}, u32[]{:S(2)}, u32[]{:S(2)}) collective-permute-start(f32[14,8,128]{2,1,0:T(8,128)S(1)} %get-tuple-element.26), channel_id=1, source_target_pairs={{0,1},{2,3},{4,5},{6,7},{1,0},{3,2},{5,4},{7,6},{8,9},{10,11},{12,... | collective-permute-start | bytes 172040 | tf_op jit(solution)/shard_map/ppermute | solution.py:644
  35.9 10.3 %all-to-all-start.1 = ((f32[32,8,128]{2,1,0:T(8,128)}), f32[32,8,128]{2,1,0:T(8,128)S(1)}, u32[]{:S(2)}, u32[]{:S(2)}) async-start(f32[32,8,128]{2,1,0:T(8,128)} %get-tuple-element.28), calls=%async_computation.1 | async-start | bytes 262144 | tf_op jit(solution)/shard_map/all_to_all | solution.py:711
